TPU v7x, 32 devices: a whole 2x2x4 slice. The times are simulated.
32 devices in a mesh: groups: 2 (over y), ep: 4 (over z), col: 4 (over x, core).
Axes of the slice: x: 2, y: 2, z: 4, core: 2. Of those that a mesh axis runs over, the one named last changes fastest.
Arguments:
- tokens: bfloat16 [128, 7168], P(('groups', 'ep')), parts along dimension 0, may hold values from -6 to 6
- routes: int32 [128, 8], P(('groups', 'ep')), parts along dimension 0, may hold values from 0 to 31, all different within a row; in each aligned block of 16 rows (0 to 15, 16 to 31, ...) at most 8 rows name the same one
- route_gates: float32 [128, 8], P(('groups', 'ep')), parts along dimension 0, may hold values from 0.05 to 1
- gate_weight: bfloat16 [32, 7168, 1024], P('ep', None, 'col'), may hold values from -0.0625 to 0.0625
- down_weight: bfloat16 [32, 1024, 7168], P('ep', 'col'), may hold values from -0.25 to 0.25
Outputs:
- mixed: bfloat16 [128, 7168], P(('groups', 'ep'), 'col'), parts along dimension 0
There are 2 independent parts, one for each index of `groups`. A program takes and returns all parts, laid end to end along the dimension named above; an argument that names none is the same for every part. Nothing has to cross between parts.
Inputs may be any that keep to these rules, and one draw needn't show every extreme that they name: `routes`: each row names 8 different experts. In each aligned block of 16 rows no expert is named by more than 8 rows, a bound that some block reaches.
All inputs are finite; a program needn't handle non-finite values.
Results may differ from a plain program's by a relative error of at most 0.013.
Values may be sent and summed in bfloat16 or wider, within the bound.
A program may use at most 192 MiB of HBM per device.

v0:
```python
import jax
import jax.numpy as jnp
from jax import lax
from jax.sharding import PartitionSpec as P

CAP = 8


def on_device(tokens, routes, route_gates, gate_weight, down_weight):
    tok_rows, model_width = tokens.shape
    top_count = routes.shape[1]
    local_experts = gate_weight.shape[0]
    owners = lax.axis_size("ep")
    experts_all = local_experts * owners
    flat_routes = routes.reshape(-1)
    onehot = (flat_routes[:, None] == jnp.arange(experts_all, dtype=jnp.int32)[None, :]).astype(
        jnp.int32
    )
    earlier = jnp.cumsum(onehot, axis=0) - onehot
    slot_index = jnp.sum(earlier * onehot, axis=1)
    position = flat_routes * CAP + slot_index
    match_table = (
        position.reshape(tok_rows, top_count)[None, :, :]
        == jnp.arange(experts_all * CAP, dtype=jnp.int32)[:, None, None]
    )
    select = jnp.any(match_table, axis=2).astype(jnp.bfloat16)
    outgoing = jnp.dot(select, tokens, preferred_element_type=jnp.float32).astype(jnp.bfloat16)
    outgoing = outgoing.reshape(experts_all, CAP, model_width)
    slot_block = lax.all_to_all(outgoing, "ep", split_axis=0, concat_axis=0, tiled=True)
    item_count = slot_block.shape[1]
    grouped = slot_block.reshape(owners, local_experts, item_count, model_width)
    hidden = jax.nn.silu(
        jnp.einsum("sjid,jdh->sjih", grouped, gate_weight, preferred_element_type=jnp.float32)
    ).astype(jnp.bfloat16)
    partial_value = jnp.einsum(
        "sjih,jhd->sjid", hidden, down_weight, preferred_element_type=jnp.float32
    ).astype(jnp.bfloat16)
    partial_value = partial_value.reshape(owners * local_experts, item_count, model_width)
    returned = lax.all_to_all(partial_value, "ep", split_axis=0, concat_axis=0, tiled=True)
    flat_rows = returned.reshape(experts_all * CAP, returned.shape[2])
    picked = jnp.take(flat_rows, position, axis=0).reshape(tok_rows, top_count, returned.shape[2])
    mixed_rows = jnp.sum(route_gates[:, :, None] * picked.astype(jnp.float32), axis=1)
    result = lax.psum_scatter(
        mixed_rows.astype(jnp.bfloat16), "col", scatter_dimension=1, tiled=True
    )
    return result


def solution(mesh):
    in_specs = (
        P(("groups", "ep"), None),
        P(("groups", "ep"), None),
        P(("groups", "ep"), None),
        P("ep", None, "col"),
        P("ep", "col", None),
    )
    out_specs = P(("groups", "ep"), "col")
    return jax.shard_map(
        on_device, mesh=mesh, in_specs=in_specs, out_specs=out_specs, check_vma=False
    )
```

profile of v0, /device:TPU:0, one launch (start us, length us, event | category | flops | bytes accessed | tf_op | source)
XLA Modules:
  0.0 249.2 jit_solution(10610282815333233304)
XLA Ops:
  6.5 0.0 copy-start
  6.5 0.8 copy.15
  7.3 0.1 reshape.65
  7.4 0.1 fusion.27
  7.5 0.2 reduce_window_sum.11
  7.7 0.2 select_reduce_fusion
  7.9 0.1 reduce_sum.23
  8.0 0.1 fusion.26
  8.1 0.0 copy-done
  8.1 1.1 fusion.7
  9.3 88.1 %all_to_all.10 = bf16[32,8,7168]{2,1,0:T(8,128)(2,1)} all-to-all(bf16[32,8,7168]{2,1,0:T(8,128)(2,1)S(1)} %fusion.7), channel_id=1, replica_groups=mesh['groups'=2,'ep'=4,'col'=4] {'ep'}, dimensions={0} | all-to-all | bytes 7340032 | tf_op jit(solution)/shard_map/all_to_all | solution.py:29
  97.4 27.7 %fusion.8 = bf16[4,8,8,7168]{3,2,0,1:T(8,128)(2,1)} fusion(bf16[8,256,7168]{2,1,0:T(8,128)(2,1)} %param.9, bf16[8,7168,256]{2,1,0:T(8,128)(2,1)} %param.8, bf16[4,8,8,7168]{3,2,1,0:T(8,128)(2,1)} %bitcast.46), kind=kOutput, calls=%fused_computation.8 | convolution fusion | flops 1881210880 | bytes 66060288 | tf_op jit(solution)/shard_map/sjih,jhd->sjid/dot_general | solution.py:35
  125.1 4.2 %copy.18 = bf16[4,8,8,7168]{3,2,1,0:T(8,128)(2,1)} copy(bf16[4,8,8,7168]{3,2,0,1:T(8,128)(2,1)} %fusion.8) | data formatting | bytes 7340032 | tf_op jit(solution)/shard_map/convert_element_type | solution.py:37
  129.3 0.0 copy-start.2
  129.3 4.9 %all-to-all-start.1 = ((bf16[32,8,7168]{2,1,0:T(8,128)(2,1)}), bf16[32,8,7168]{2,1,0:T(8,128)(2,1)}, u32[]{:S(2)}, u32[]{:S(2)}) async-start(bf16[32,8,7168]{2,1,0:T(8,128)(2,1)} %bitcast.45), calls=%async_computation.1 | async-start | bytes 7340032 | tf_op jit(solution)/shard_map/all_to_all | solution.py:39
  134.2 0.0 reduce-scatter.2.cloned.1.call-start
  134.2 0.1 mul.41
  134.3 0.0 copy-done.2
  134.3 0.1 copy.14
  134.4 80.9 %all-to-all-done.1 = bf16[32,8,7168]{2,1,0:T(8,128)(2,1)} async-done(((bf16[32,8,7168]{2,1,0:T(8,128)(2,1)}), bf16[32,8,7168]{2,1,0:T(8,128)(2,1)}, u32[]{:S(2)}, u32[]{:S(2)}) %all-to-all-start.1) | async-done | bytes 3670048 | tf_op jit(solution)/shard_map/all_to_all | solution.py:39
  215.3 0.0 copy-start.1
  215.3 5.9 %gather_fusion = bf16[128,7168]{1,0:T(8,128)(2,1)S(1)} fusion(bf16[256,7168]{1,0:T(8,128)(2,1)} %bitcast.9, s32[1024]{0:T(1024)S(1)} %pad_clamp_fusion), kind=kCustom, calls=%fused_computation | custom fusion | bytes 3670528 | tf_op jit(solution)/shard_map/jit(_take)/gather | solution.py:41
  221.2 2.0 multiply_reduce_fusion
  223.2 0.0 reduce-scatter.2.cloned.1.call-update
  223.2 19.2 %reduce-scatter.2.cloned.1.call-done = bf16[16,1792]{1,0:T(8,128)(2,1)} async-done(((bf16[16,7168]{1,0:T(8,128)(2,1)}), bf16[16,1792]{1,0:T(8,128)(2,1)}) %reduce-scatter.2.cloned.1.call-update) | async-done | bytes 57360 | tf_op jit(solution)/shard_map/reduce_scatter | solution.py:43
  242.4 0.0 copy-done.1
  (4 shorter events, 0.0 us)
Async XLA Ops:
  6.5 1.6 copy-start
  129.3 5.0 %copy-start.2 = (f32[16,8]{0,1:T(8,128)S(1)}, f32[16,8]{0,1:T(8,128)}, u32[]{:S(2)}) copy-start(f32[16,8]{0,1:T(8,128)} %param.7) | copy-start | bytes 1540
  129.3 86.0 %all-to-all-start.1 = ((bf16[32,8,7168]{2,1,0:T(8,128)(2,1)}), bf16[32,8,7168]{2,1,0:T(8,128)(2,1)}, u32[]{:S(2)}, u32[]{:S(2)}) async-start(bf16[32,8,7168]{2,1,0:T(8,128)(2,1)} %bitcast.45), calls=%async_computation.1 | async-start | bytes 7340032 | tf_op jit(solution)/shard_map/all_to_all | solution.py:39
  134.2 108.2 %reduce-scatter.2.cloned.1.call-start = ((), (), s32[]{:S(2)}) async-start(), calls=%async_computation.3 | async-start | bytes 286720 | tf_op jit(solution)/shard_map/reduce_scatter | solution.py:43
  215.3 27.1 %copy-start.1 = (bf16[16,7168]{1,0:T(8,128)(2,1)S(1)}, bf16[16,7168]{1,0:T(8,128)(2,1)}, u32[]{:S(2)}) copy-start(bf16[16,7168]{1,0:T(8,128)(2,1)} %param.5) | copy-start | bytes 688132
Sparse Core Ops, SparseCore 0:
  223.3 18.9 reduce-scatter.1
where the time goes:
time: 250 us; the launch traced here: 249 us
  waiting for transfers between devices  100 us (40%)
  blocking collectives  88.1 us (35%)
  matrix products  28.9 us (12%)
  between operations  13.5 us (5%)
  local copies, waits for them, and re-layouts  11.2 us (4%)
  starting transfers between devices  4.91 us (2%)
  other arithmetic  2.6 us (1%)
    all_to_all x1, blocking collectives, on_device(): lax.all_to_all(outgoing, 'ep', split_axis=0, concat_axis=0, tiled=True)  88.1 us
    all_to_all x1, waiting for transfers between devices, on_device(): lax.all_to_all(partial_value, 'ep', split_axis=0, concat_axis=0, tiled=True)  80.9 us
    dot_general x1, matrix products, on_device(): jnp.einsum('sjih,jhd->sjid', hidden, down_weight, preferred_element_type=...  27.7 us
    reduce_scatter x1, waiting for transfers between devices, on_device(): lax.psum_scatter(mixed_rows.astype(jnp.bfloat16), 'col', scatter_dimensio...  19.2 us
    gather x1, local copies, waits for them, and re-layouts, on_device(): jnp.take(flat_rows, position, axis=0)  5.92 us
  transfers between devices with their start and end apart: 2, of which 2 were waited for; matrix products, arithmetic and copies ran while one was open for 0% of the time, Pallas kernels for 0%

commit v1 on v0

v1 whole, which is shorter than its diff:
```python
import functools

import jax
import jax.numpy as jnp
from jax import lax
from jax.experimental import pallas as pl
from jax.experimental.pallas import tpu as pltpu
from jax.sharding import PartitionSpec as P

MESH = pl.DeviceIdType.MESH
AHEAD = 2


def kernel(
    n_ep, n_col, width,
    tok_hbm, routes_ref, gates_ref, wg_hbm, wd_hbm, out_ref,
    tok_all, g_all, wg_buf, wd_buf, h_buf, part, sbuf, rbuf, zsend, zown, zrecv,
    tok_sem, wg_sem, wd_sem, tz_send, tz_recv, gz_send, gz_recv,
    tc_send, tc_recv, rc_send, rc_recv, rz_send, rz_recv,
):
    rows, depth = tok_hbm.shape
    quarter = depth // n_col
    local_experts, hid = wg_buf.shape[0], wg_buf.shape[2]
    chunks = wd_buf.shape[0]
    lanes = g_all.shape[1]
    total = tok_all.shape[0]
    bits = []
    while (1 << len(bits)) < n_col:
        bits.append(1 << len(bits))
    me = lax.axis_index("ep")
    col = lax.axis_index("col")

    def low(k):
        return k & -k if k else n_col

    def partner(bit):
        return col + bit - 2 * bit * lax.rem(lax.div(col, bit), 2)

    def piece(k):
        p = col
        for bit in bits:
            if k & bit:
                p = p + bit - 2 * bit * lax.rem(lax.div(col, bit), 2)
        return p

    def block(index):
        return pl.ds(pl.multiple_of(index * rows, rows), rows)

    def columns(k):
        return pl.ds(pl.multiple_of(piece(k) * quarter, 128), quarter)

    def wg_copy(e):
        return pltpu.make_async_copy(wg_hbm.at[e], wg_buf.at[e], wg_sem.at[e])

    def wd_copy(j, k):
        at = pl.ds(pl.multiple_of(piece(k) * quarter + j * width, 128), width)
        return pltpu.make_async_copy(
            wd_hbm.at[:, :, at], wd_buf.at[j, k], wd_sem.at[j, k]
        )

    def wd_start(j):
        for k in range(n_col):
            wd_copy(j, k).start()

    def tok_z(d):
        return pltpu.make_async_remote_copy(
            src_ref=tok_hbm.at[:, columns(0)],
            dst_ref=tok_all.at[block(me), columns(0)],
            send_sem=tz_send.at[d], recv_sem=tz_recv.at[d],
            device_id={"ep": lax.rem(me + d, n_ep)}, device_id_type=MESH,
        )

    def gate_z(d):
        return pltpu.make_async_remote_copy(
            src_ref=g_all.at[block(me)], dst_ref=g_all.at[block(me)],
            send_sem=gz_send.at[d], recv_sem=gz_recv.at[d],
            device_id={"ep": lax.rem(me + d, n_ep)}, device_id_type=MESH,
        )

    def tok_c(d, k, bit):
        view = tok_all.at[block(lax.rem(me - d + n_ep, n_ep)), columns(k)]
        return pltpu.make_async_remote_copy(
            src_ref=view, dst_ref=view,
            send_sem=tc_send.at[d, k | bit], recv_sem=tc_recv.at[d, k | bit],
            device_id={"col": partner(bit)}, device_id_type=MESH,
        )

    def red_c(j, k):
        return pltpu.make_async_remote_copy(
            src_ref=sbuf.at[j, k - 1], dst_ref=rbuf.at[j, k - 1],
            send_sem=rc_send.at[j, k], recv_sem=rc_recv.at[j, k],
            device_id={"col": partner(low(k))}, device_id_type=MESH,
        )

    def red_z(j, d):
        return pltpu.make_async_remote_copy(
            src_ref=zsend.at[j, lax.rem(me + d, n_ep)], dst_ref=zrecv.at[j, d - 1],
            send_sem=rz_send.at[j, d], recv_sem=rz_recv.at[j, d],
            device_id={"ep": lax.rem(me + d, n_ep)}, device_id_type=MESH,
        )

    def each(lo, hi, body):
        def step(i, carry):
            body(i)
            return carry
        lax.fori_loop(lo, hi, step, 0)

    own_copy = pltpu.make_async_copy(tok_hbm, tok_all.at[block(me)], tok_sem)
    own_copy.start()
    wg_copy(0).start()

    barrier = pltpu.get_barrier_semaphore()
    each(1, n_ep, lambda d: pl.semaphore_signal(
        barrier, inc=1, device_id={"ep": lax.rem(me + d, n_ep)}, device_id_type=MESH))
    for bit in bits:
        pl.semaphore_signal(
            barrier, inc=1, device_id={"col": partner(bit)}, device_id_type=MESH)

    expert = lax.broadcasted_iota(jnp.int32, (rows, lanes), 1)
    dense = jnp.zeros((rows, lanes), jnp.float32)
    for k in range(routes_ref.shape[1]):
        dense = dense + jnp.where(
            routes_ref[:, k : k + 1] == expert, gates_ref[:, k : k + 1], 0.0)
    g_all[block(me), :] = dense

    pl.semaphore_wait(barrier, n_ep - 1 + len(bits))

    each(1, n_ep, lambda d: tok_z(d).start())
    each(1, n_ep, lambda d: gate_z(d).start())
    each(1, local_experts, lambda e: wg_copy(e).start())
    each(0, min(AHEAD, chunks), wd_start)

    def arrived(d):
        tok_z(d).wait_recv()
        for bit in reversed(bits):
            tok_c(d, 0, bit).start()

    each(1, n_ep, arrived)
    for bit in reversed(bits):
        higher = [k for k in range(1, n_col) if low(k) == bit]

        def relay(d):
            for k in higher:
                tok_c(d, k ^ bit, bit).wait_recv()
                for b in reversed(bits):
                    if b < bit:
                        tok_c(d, k, b).start()

        each(1, n_ep, relay)
    each(1, n_ep, lambda d: gate_z(d).wait_recv())
    own_copy.wait()

    def up(e):
        wg_copy(e).wait()

        @pl.when(e + AHEAD < chunks)
        def _():
            wd_start(e + AHEAD)

        v = jnp.dot(tok_all[...], wg_buf[e], preferred_element_type=jnp.float32)
        mine = lax.broadcasted_iota(jnp.int32, (total, lanes), 1) == me * local_experts + e
        weight = jnp.sum(jnp.where(mine, g_all[...], 0.0), axis=1, keepdims=True)
        h = v / (1.0 + jnp.exp(-v))
        h_buf[:, pl.ds(pl.multiple_of(e * hid, 128), hid)] = (h * weight).astype(h_buf.dtype)

    each(0, local_experts, up)
    each(min(local_experts + AHEAD, chunks), chunks, wd_start)

    order = [k for k in range(n_col) if k & 1] + [k for k in range(n_col) if not k & 1]
    if n_col == 1:
        order = [0]

    def down(j):
        for k in order:
            wd_copy(j, k).wait()
            y = jnp.dot(
                h_buf[...], wd_buf[j, k].reshape(local_experts * hid, width),
                preferred_element_type=jnp.float32)
            if k & 1:
                sbuf[j, k - 1] = y.astype(sbuf.dtype)
                red_c(j, k).start()
            else:
                part[j, k // 2] = y

    def reduce_stage(j, bit):
        for k in reversed(range(0, n_col, 2 * bit)):
            red_c(j, k | bit).wait_recv()
            y = part[j, k // 2] + rbuf[j, (k | bit) - 1].astype(jnp.float32)
            if k and low(k) == 2 * bit:
                sbuf[j, k - 1] = y.astype(sbuf.dtype)
                red_c(j, k).start()
            elif k or 2 * bit < n_col:
                part[j, k // 2] = y
            else:
                finish(j, y)

    def finish(j, y):
        part[j, 0] = y
        zsend[j] = y.astype(zsend.dtype).reshape(n_ep, rows, width)
        zown[j] = part[j, 0, block(me), :]
        each(1, n_ep, lambda d: red_z(j, d).start())

    def step(t):
        @pl.when(t < chunks)
        def _():
            down(t)

        for i, bit in enumerate(bits):
            j = t - 1 - i

            @pl.when((j >= 0) & (j < chunks))
            def _():
                reduce_stage(j, bit)

    each(0, chunks + len(bits), step)

    def last(j):
        def add(d, y):
            red_z(j, d).wait_recv()
            return y + zrecv[j, d - 1].astype(jnp.float32)

        y = lax.fori_loop(1, n_ep, add, zown[j])
        out_ref[:, pl.ds(pl.multiple_of(j * width, 128), width)] = y.astype(out_ref.dtype)

    each(0, chunks, last)

    def sent(d):
        tok_z(d).wait_send()
        gate_z(d).wait_send()
        for k in range(1, n_col):
            tok_c(d, k ^ low(k), low(k)).wait_send()

    each(1, n_ep, sent)

    def sent_chunk(j):
        for k in range(1, n_col):
            red_c(j, k).wait_send()
        each(1, n_ep, lambda d: red_z(j, d).wait_send())

    each(0, chunks, sent_chunk)


def on_device(tokens, routes, route_gates, gate_weight, down_weight):
    rows, depth = tokens.shape
    local_experts, _, hid = gate_weight.shape
    n_ep, n_col = lax.axis_size("ep"), lax.axis_size("col")
    quarter = depth // n_col
    width = 256 if quarter % 256 == 0 else 128
    chunks = quarter // width
    total = n_ep * rows
    lanes = -(-local_experts * n_ep // 128) * 128
    bf16, f32 = jnp.bfloat16, jnp.float32
    dma = pltpu.SemaphoreType.DMA
    vmem = pl.BlockSpec(memory_space=pltpu.VMEM)
    hbm = pl.BlockSpec(memory_space=pl.ANY)
    flops = 4 * total * depth * local_experts * hid
    return pl.pallas_call(
        functools.partial(kernel, n_ep, n_col, width),
        out_shape=jax.ShapeDtypeStruct((rows, quarter), tokens.dtype),
        in_specs=[hbm, vmem, vmem, hbm, hbm],
        out_specs=vmem,
        scratch_shapes=[
            pltpu.VMEM((total, depth), bf16),
            pltpu.VMEM((total, lanes), f32),
            pltpu.VMEM((local_experts, depth, hid), bf16),
            pltpu.VMEM((chunks, n_col, local_experts, hid, width), bf16),
            pltpu.VMEM((total, local_experts * hid), bf16),
            pltpu.VMEM((chunks, max(1, n_col // 2), total, width), f32),
            pltpu.VMEM((chunks, n_col - 1, total, width), bf16),
            pltpu.VMEM((chunks, n_col - 1, total, width), bf16),
            pltpu.VMEM((chunks, n_ep, rows, width), bf16),
            pltpu.VMEM((chunks, rows, width), f32),
            pltpu.VMEM((chunks, n_ep - 1, rows, width), bf16),
            dma,
            dma((local_experts,)),
            dma((chunks, n_col)),
            dma((n_ep,)), dma((n_ep,)), dma((n_ep,)), dma((n_ep,)),
            dma((n_ep, n_col)), dma((n_ep, n_col)),
            dma((chunks, n_col)), dma((chunks, n_col)),
            dma((chunks, n_ep)), dma((chunks, n_ep)),
        ],
        compiler_params=pltpu.CompilerParams(
            collective_id=0, has_side_effects=True, vmem_limit_bytes=63 * 1024 * 1024
        ),
        cost_estimate=pl.CostEstimate(
            flops=flops, bytes_accessed=4 * local_experts * depth * hid, transcendentals=0
        ),
    )(tokens, routes, route_gates, gate_weight, down_weight)


def solution(mesh):
    in_specs = (
        P(("groups", "ep"), None),
        P(("groups", "ep"), None),
        P(("groups", "ep"), None),
        P("ep", None, "col"),
        P("ep", "col", None),
    )
    out_specs = P(("groups", "ep"), "col")
    return jax.shard_map(
        on_device, mesh=mesh, in_specs=in_specs, out_specs=out_specs, check_vma=False
    )
```

time: 250 us -> 52.5 us (0.21)
  waiting for transfers between devices: 100 us -> 0 us
  blocking collectives: 88.1 us -> 0 us
  Pallas kernels: 0 us -> 48 us
  matrix products: 28.9 us -> 0 us
  between operations: 13.5 us -> 0.01 us
  local copies, waits for them, and re-layouts: 11.2 us -> 4.15 us
  starting transfers between devices: 4.91 us -> 0 us
  other arithmetic: 2.6 us -> 0 us
    all_to_all x1 -> x0, blocking collectives: 88.1 us -> none  [on_device(): lax.all_to_all(outgoing, 'ep', split_axis=0, concat_axis=0, tiled=True)]
    all_to_all x1 -> x0, waiting for transfers between devices: 80.9 us -> none  [on_device(): lax.all_to_all(partial_value, 'ep', split_axis=0, concat_axis=0, tiled=True)]
    pallas_call x0 -> x1, Pallas kernels: none -> 48 us  [on_device(): pl.pallas_call(functools.partial(kernel, n_ep, n_col, width), out_shape=j...]
    dot_general x2 -> x0, matrix products: 28.9 us -> none  [the longest x1 27.7 us: on_device(): jnp.einsum('sjih,jhd->sjid', hidden, down_weight, preferred_element_type=...]
    reduce_scatter x1 -> x0, waiting for transfers between devices: 19.2 us -> none  [on_device(): lax.psum_scatter(mixed_rows.astype(jnp.bfloat16), 'col', scatter_dimensio...]
    gather x1 -> x0, local copies, waits for them, and re-layouts: 5.92 us -> none  [on_device(): jnp.take(flat_rows, position, axis=0)]
    all_to_all x1 -> x0, starting transfers between devices: 4.87 us -> none  [on_device(): lax.all_to_all(partial_value, 'ep', split_axis=0, concat_axis=0, tiled=True)]
    convert_element_type x1 -> x0, local copies, waits for them, and re-layouts: 4.15 us -> none  [on_device(): partial_value = jnp.einsum('sjih,jhd->sjid', hidden, down_weight, preferr...]
  transfers between devices with their start and end apart: 2 -> 0, of which waited for: 2 -> 0; matrix products, arithmetic and copies ran while one was open for 0% -> 0% of each run, Pallas kernels for 0% -> 0%
where the time goes in v1:
time: 52.5 us; the launch traced here: 52.2 us
  Pallas kernels  48 us (91%)
  local copies, waits for them, and re-layouts  4.15 us (8%)
    pallas_call x1, Pallas kernels, on_device(): pl.pallas_call(functools.partial(kernel, n_ep, n_col, width), out_shape=j...  48 us
    unnamed x3, local copies, waits for them, and re-layouts  4.15 us

profile of v1, /device:TPU:0, one launch (start us, length us, event | category | flops | bytes accessed | tf_op | source)
XLA Modules:
  0.0 52.2 jit_solution(7030403306798571544)
XLA Ops:
  0.0 1.4 %copy.6.routes_ref = s32[16,8]{1,0:T(8,128)} copy(s32[16,8]{0,1:T(8,128)} %param.6) | data formatting | bytes 1024 | tf_op args[1]
  1.4 1.3 %copy.7.gates_ref = f32[16,8]{1,0:T(8,128)} copy(f32[16,8]{0,1:T(8,128)} %param.7) | data formatting | bytes 1024 | tf_op args[2]
  2.7 48.0 %shard_map.55 = bf16[16,1792]{1,0:T(8,128)(2,1)} custom-call(bf16[16,7168]{1,0:T(8,128)(2,1)} %tok_hbm.1, s32[16,8]{1,0:T(8,128)} %copy.6.routes_ref, f32[16,8]{1,0:T(8,128)} %copy.7.gates_ref, bf16[8,7168,256]{2,1,0:T(8,128)(2,1)} %wg_hbm.1, bf16[8,256,7168]{2,1,0:T(8,128)(2,1)} %wd_hbm.1), custom_call_target="tpu_custom_call" | custom-call | flops 3758096384 | bytes 58720256 | tf_op jit(solution)/shard_map/pallas_call | solution.py:257
  50.8 1.4 %copy.9 = bf16[16,1792]{1,0:T(8,128)(2,1)} copy(bf16[16,1792]{1,0:T(8,128)(2,1)} %shard_map.55) | data formatting | bytes 114688

commit v2 on v1

--- a/solution.py
+++ b/solution.py
@@ -9,18 +9,19 @@
 
 MESH = pl.DeviceIdType.MESH
 AHEAD = 2
+LAG = 2
 
 
 def kernel(
     n_ep, n_col, width,
     tok_hbm, routes_ref, gates_ref, wg_hbm, wd_hbm, out_ref,
-    tok_all, g_all, wg_buf, wd_buf, h_buf, part, sbuf, rbuf, zsend, zown, zrecv,
+    tok_all, g_all, turn, acc, wg_buf, wd_buf, h_buf, part, sbuf, rbuf, zsend, zown, zrecv,
     tok_sem, wg_sem, wd_sem, tz_send, tz_recv, gz_send, gz_recv,
     tc_send, tc_recv, rc_send, rc_recv, rz_send, rz_recv,
 ):
     rows, depth = tok_hbm.shape
     quarter = depth // n_col
-    local_experts, hid = wg_buf.shape[0], wg_buf.shape[2]
+    local_experts, hid = wg_buf.shape[1], wg_buf.shape[3]
     chunks = wd_buf.shape[0]
     lanes = g_all.shape[1]
     total = tok_all.shape[0]
@@ -49,8 +50,10 @@
     def columns(k):
         return pl.ds(pl.multiple_of(piece(k) * quarter, 128), quarter)
 
-    def wg_copy(e):
-        return pltpu.make_async_copy(wg_hbm.at[e], wg_buf.at[e], wg_sem.at[e])
+    def wg_copy(k, e):
+        return pltpu.make_async_copy(
+            wg_hbm.at[e, columns(k)], wg_buf.at[k, e], wg_sem.at[k, e]
+        )
 
     def wd_copy(j, k):
         at = pl.ds(pl.multiple_of(piece(k) * quarter + j * width, 128), width)
@@ -104,10 +107,6 @@
             body(i)
             return carry
         lax.fori_loop(lo, hi, step, 0)
-
-    own_copy = pltpu.make_async_copy(tok_hbm, tok_all.at[block(me)], tok_sem)
-    own_copy.start()
-    wg_copy(0).start()
 
     barrier = pltpu.get_barrier_semaphore()
     each(1, n_ep, lambda d: pl.semaphore_signal(
@@ -116,55 +115,59 @@
         pl.semaphore_signal(
             barrier, inc=1, device_id={"col": partner(bit)}, device_id_type=MESH)
 
-    expert = lax.broadcasted_iota(jnp.int32, (rows, lanes), 1)
-    dense = jnp.zeros((rows, lanes), jnp.float32)
-    for k in range(routes_ref.shape[1]):
+    own_copy = pltpu.make_async_copy(tok_hbm, tok_all.at[block(me)], tok_sem)
+    own_copy.start()
+    each(0, local_experts, lambda e: wg_copy(0, e).start())
+
+    expert = lax.broadcasted_iota(jnp.int32, (lanes, rows), 0)
+    dense = jnp.zeros((lanes, rows), jnp.float32)
+    for k in range(routes_ref.shape[0]):
         dense = dense + jnp.where(
-            routes_ref[:, k : k + 1] == expert, gates_ref[:, k : k + 1], 0.0)
-    g_all[block(me), :] = dense
+            routes_ref[k : k + 1, :] == expert, gates_ref[k : k + 1, :], 0.0)
+    turn[...] = jnp.zeros_like(turn)
+    turn[:, :rows] = dense
+    g_all[block(me), :] = turn[...].T[:rows]
 
     pl.semaphore_wait(barrier, n_ep - 1 + len(bits))
 
     each(1, n_ep, lambda d: tok_z(d).start())
     each(1, n_ep, lambda d: gate_z(d).start())
-    each(1, local_experts, lambda e: wg_copy(e).start())
+    for k in range(1, n_col):
+        each(0, local_experts, lambda e: wg_copy(k, e).start())
     each(0, min(AHEAD, chunks), wd_start)
 
-    def arrived(d):
-        tok_z(d).wait_recv()
-        for bit in reversed(bits):
-            tok_c(d, 0, bit).start()
-
-    each(1, n_ep, arrived)
-    for bit in reversed(bits):
-        higher = [k for k in range(1, n_col) if low(k) == bit]
-
-        def relay(d):
-            for k in higher:
-                tok_c(d, k ^ bit, bit).wait_recv()
-                for b in reversed(bits):
-                    if b < bit:
-                        tok_c(d, k, b).start()
-
-        each(1, n_ep, relay)
-    each(1, n_ep, lambda d: gate_z(d).wait_recv())
-    own_copy.wait()
-
-    def up(e):
-        wg_copy(e).wait()
-
-        @pl.when(e + AHEAD < chunks)
-        def _():
-            wd_start(e + AHEAD)
-
-        v = jnp.dot(tok_all[...], wg_buf[e], preferred_element_type=jnp.float32)
+    def up(k, e):
+        wg_copy(k, e).wait()
+        v = jnp.dot(tok_all[:, columns(k)], wg_buf[k, e], preferred_element_type=jnp.float32)
+        if k:
+            v = v + acc[e]
+        if k < n_col - 1:
+            acc[e] = v
+            return
         mine = lax.broadcasted_iota(jnp.int32, (total, lanes), 1) == me * local_experts + e
         weight = jnp.sum(jnp.where(mine, g_all[...], 0.0), axis=1, keepdims=True)
         h = v / (1.0 + jnp.exp(-v))
         h_buf[:, pl.ds(pl.multiple_of(e * hid, 128), hid)] = (h * weight).astype(h_buf.dtype)
 
-    each(0, local_experts, up)
-    each(min(local_experts + AHEAD, chunks), chunks, wd_start)
+    for k in range(n_col):
+        def arrived(d):
+            if k:
+                tok_c(d, k ^ low(k), low(k)).wait_recv()
+            else:
+                tok_z(d).wait_recv()
+            for bit in reversed(bits):
+                if bit < low(k):
+                    tok_c(d, k, bit).start()
+
+        each(1, n_ep, arrived)
+        if k == 0:
+            own_copy.wait()
+        if k == n_col - 1:
+            each(1, n_ep, lambda d: gate_z(d).wait_recv())
+        each(0, local_experts, functools.partial(up, k))
+        for j in range(AHEAD + k * chunks // n_col, AHEAD + (k + 1) * chunks // n_col):
+            if j < chunks:
+                wd_start(j)
 
     order = [k for k in range(n_col) if k & 1] + [k for k in range(n_col) if not k & 1]
     if n_col == 1:
@@ -206,13 +209,13 @@
             down(t)
 
         for i, bit in enumerate(bits):
-            j = t - 1 - i
+            j = t - LAG * (i + 1)
 
             @pl.when((j >= 0) & (j < chunks))
             def _():
                 reduce_stage(j, bit)
 
-    each(0, chunks + len(bits), step)
+    each(0, chunks + LAG * len(bits), step)
 
     def last(j):
         def add(d, y):
@@ -262,7 +265,9 @@
         scratch_shapes=[
             pltpu.VMEM((total, depth), bf16),
             pltpu.VMEM((total, lanes), f32),
-            pltpu.VMEM((local_experts, depth, hid), bf16),
+            pltpu.VMEM((lanes, 128), f32),
+            pltpu.VMEM((local_experts, total, hid), f32),
+            pltpu.VMEM((n_col, local_experts, quarter, hid), bf16),
             pltpu.VMEM((chunks, n_col, local_experts, hid, width), bf16),
             pltpu.VMEM((total, local_experts * hid), bf16),
             pltpu.VMEM((chunks, max(1, n_col // 2), total, width), f32),
@@ -272,7 +277,7 @@
             pltpu.VMEM((chunks, rows, width), f32),
             pltpu.VMEM((chunks, n_ep - 1, rows, width), bf16),
             dma,
-            dma((local_experts,)),
+            dma((n_col, local_experts)),
             dma((chunks, n_col)),
             dma((n_ep,)), dma((n_ep,)), dma((n_ep,)), dma((n_ep,)),
             dma((n_ep, n_col)), dma((n_ep, n_col)),
@@ -285,7 +290,7 @@
         cost_estimate=pl.CostEstimate(
             flops=flops, bytes_accessed=4 * local_experts * depth * hid, transcendentals=0
         ),
-    )(tokens, routes, route_gates, gate_weight, down_weight)
+    )(tokens, routes.T, route_gates.T, gate_weight, down_weight)
 
 
 def solution(mesh):

time: 52.5 us -> 47.4 us (0.903)
  local copies, waits for them, and re-layouts: 4.15 us -> 1.45 us
  Pallas kernels: 48 us -> 45.8 us
    unnamed x3 -> x1, local copies, waits for them, and re-layouts: 4.15 us -> 1.45 us
    pallas_call x1, Pallas kernels: 48 us -> 45.8 us  [on_device(): pl.pallas_call(functools.partial(kernel, n_ep, n_col, width), out_shape=j...]
where the time goes in v2:
time: 47.4 us; the launch traced here: 47.2 us
  Pallas kernels  45.8 us (97%)
  local copies, waits for them, and re-layouts  1.45 us (3%)
    pallas_call x1, Pallas kernels, on_device(): pl.pallas_call(functools.partial(kernel, n_ep, n_col, width), out_shape=j...  45.8 us
    unnamed x1, local copies, waits for them, and re-layouts  1.45 us

profile of v2, /device:TPU:0, one launch (start us, length us, event | category | flops | bytes accessed | tf_op | source)
XLA Modules:
  0.0 47.2 jit_solution(5906056030370692497)
XLA Ops:
  0.0 45.8 %shard_map.55 = bf16[16,1792]{1,0:T(8,128)(2,1)} custom-call(bf16[16,7168]{1,0:T(8,128)(2,1)} %tok_hbm.1, s32[8,16]{1,0:T(8,128)} %bitcast.2, f32[8,16]{1,0:T(8,128)} %bitcast.3, bf16[8,7168,256]{2,1,0:T(8,128)(2,1)} %wg_hbm.1, bf16[8,256,7168]{2,1,0:T(8,128)(2,1)} %wd_hbm.1), custom_call_target="tpu_custom_call" | custom-call | flops 3758096384 | bytes 58720256 | tf_op jit(solution)/shard_map/pallas_call | solution.py:260
  45.8 1.4 %copy.7 = bf16[16,1792]{1,0:T(8,128)(2,1)} copy(bf16[16,1792]{1,0:T(8,128)(2,1)} %shard_map.55) | data formatting | bytes 114688

commit v3 on v2

--- a/solution.py
+++ b/solution.py
@@ -9,7 +9,8 @@
 
 MESH = pl.DeviceIdType.MESH
 AHEAD = 2
-LAG = 2
+LAG = 4
+BATCH = 8
 
 
 def kernel(
@@ -137,7 +138,6 @@
     each(0, min(AHEAD, chunks), wd_start)
 
     def up(k, e):
-        wg_copy(k, e).wait()
         v = jnp.dot(tok_all[:, columns(k)], wg_buf[k, e], preferred_element_type=jnp.float32)
         if k:
             v = v + acc[e]
@@ -149,6 +149,14 @@
         h = v / (1.0 + jnp.exp(-v))
         h_buf[:, pl.ds(pl.multiple_of(e * hid, 128), hid)] = (h * weight).astype(h_buf.dtype)
 
+    batch = BATCH if local_experts % BATCH == 0 else 1
+
+    def up_batch(k, i):
+        for m in range(batch):
+            wg_copy(k, i * batch + m).wait()
+        for m in range(batch):
+            up(k, i * batch + m)
+
     for k in range(n_col):
         def arrived(d):
             if k:
@@ -164,7 +172,7 @@
             own_copy.wait()
         if k == n_col - 1:
             each(1, n_ep, lambda d: gate_z(d).wait_recv())
-        each(0, local_experts, functools.partial(up, k))
+        each(0, local_experts // batch, functools.partial(up_batch, k))
         for j in range(AHEAD + k * chunks // n_col, AHEAD + (k + 1) * chunks // n_col):
             if j < chunks:
                 wd_start(j)
@@ -176,14 +184,17 @@
     def down(j):
         for k in order:
             wd_copy(j, k).wait()
+        for k in order:
             y = jnp.dot(
                 h_buf[...], wd_buf[j, k].reshape(local_experts * hid, width),
                 preferred_element_type=jnp.float32)
             if k & 1:
                 sbuf[j, k - 1] = y.astype(sbuf.dtype)
-                red_c(j, k).start()
             else:
                 part[j, k // 2] = y
+            if k == n_col - 1:
+                for odd in range(1, n_col, 2):
+                    red_c(j, odd).start()
 
     def reduce_stage(j, bit):
         for k in reversed(range(0, n_col, 2 * bit)):

time: 47.4 us -> 39.8 us (0.84)
  Pallas kernels: 45.8 us -> 38.2 us
    pallas_call x1, Pallas kernels: 45.8 us -> 38.2 us  [on_device(): pl.pallas_call(functools.partial(kernel, n_ep, n_col, width), out_shape=j...]
where the time goes in v3:
time: 39.8 us; the launch traced here: 39.6 us
  Pallas kernels  38.2 us (96%)
  local copies, waits for them, and re-layouts  1.45 us (4%)
    pallas_call x1, Pallas kernels, on_device(): pl.pallas_call(functools.partial(kernel, n_ep, n_col, width), out_shape=j...  38.2 us
    unnamed x1, local copies, waits for them, and re-layouts  1.45 us

profile of v3, /device:TPU:0, one launch (start us, length us, event | category | flops | bytes accessed | tf_op | source)
XLA Modules:
  0.0 39.6 jit_solution(15912238854281018679)
XLA Ops:
  0.0 38.2 %shard_map.55 = bf16[16,1792]{1,0:T(8,128)(2,1)} custom-call(bf16[16,7168]{1,0:T(8,128)(2,1)} %tok_hbm.1, s32[8,16]{1,0:T(8,128)} %bitcast.2, f32[8,16]{1,0:T(8,128)} %bitcast.3, bf16[8,7168,256]{2,1,0:T(8,128)(2,1)} %wg_hbm.1, bf16[8,256,7168]{2,1,0:T(8,128)(2,1)} %wd_hbm.1), custom_call_target="tpu_custom_call" | custom-call | flops 3758096384 | bytes 58720256 | tf_op jit(solution)/shard_map/pallas_call | solution.py:271
  38.2 1.4 %copy.7 = bf16[16,1792]{1,0:T(8,128)(2,1)} copy(bf16[16,1792]{1,0:T(8,128)(2,1)} %shard_map.55) | data formatting | bytes 114688

commit v4 on v3

--- a/solution.py
+++ b/solution.py
@@ -119,6 +119,8 @@
     own_copy = pltpu.make_async_copy(tok_hbm, tok_all.at[block(me)], tok_sem)
     own_copy.start()
     each(0, local_experts, lambda e: wg_copy(0, e).start())
+    for k in range(1, n_col):
+        each(0, local_experts, lambda e: wg_copy(k, e).start())
 
     expert = lax.broadcasted_iota(jnp.int32, (lanes, rows), 0)
     dense = jnp.zeros((lanes, rows), jnp.float32)
@@ -133,8 +135,6 @@
 
     each(1, n_ep, lambda d: tok_z(d).start())
     each(1, n_ep, lambda d: gate_z(d).start())
-    for k in range(1, n_col):
-        each(0, local_experts, lambda e: wg_copy(k, e).start())
     each(0, min(AHEAD, chunks), wd_start)
 
     def up(k, e):

time: 39.8 us -> 39.8 us (level)
  no operation moved by 1% of the time
where the time goes in v4:
time: 39.8 us; the launch traced here: 39.6 us
  Pallas kernels  38.2 us (96%)
  local copies, waits for them, and re-layouts  1.45 us (4%)
    pallas_call x1, Pallas kernels, on_device(): pl.pallas_call(functools.partial(kernel, n_ep, n_col, width), out_shape=j...  38.2 us
    unnamed x1, local copies, waits for them, and re-layouts  1.45 us

profile of v4, /device:TPU:0, one launch (start us, length us, event | category | flops | bytes accessed | tf_op | source)
XLA Modules:
  0.0 39.6 jit_solution(4230933473393720085)
XLA Ops:
  0.0 38.2 %shard_map.55 = bf16[16,1792]{1,0:T(8,128)(2,1)} custom-call(bf16[16,7168]{1,0:T(8,128)(2,1)} %tok_hbm.1, s32[8,16]{1,0:T(8,128)} %bitcast.2, f32[8,16]{1,0:T(8,128)} %bitcast.3, bf16[8,7168,256]{2,1,0:T(8,128)(2,1)} %wg_hbm.1, bf16[8,256,7168]{2,1,0:T(8,128)(2,1)} %wd_hbm.1), custom_call_target="tpu_custom_call" | custom-call | flops 3758096384 | bytes 58720256 | tf_op jit(solution)/shard_map/pallas_call | solution.py:271
  38.2 1.4 %copy.7 = bf16[16,1792]{1,0:T(8,128)(2,1)} copy(bf16[16,1792]{1,0:T(8,128)(2,1)} %shard_map.55) | data formatting | bytes 114688
